TPU v7x, 512 devices: a whole 4x4x16 slice. The times are simulated.
512 devices in a mesh: layer: 2 (over core), latent: 32 (over z_hi, y, x), token: 8 (over z_lo).
Axes of the slice: x: 4, y: 4, z: 16 (z_hi: 2, z_lo: 8; z = z_hi * 8 + z_lo), core: 2. Of those that a mesh axis runs over, the one named last changes fastest.
Arguments:
- taps: bfloat16 [2, 1792, 3584], P('layer', 'token'), may hold values from -6 to 6
- token_ids: int32 [1792], P('token'), may hold values from 2 to 255999, as said below
- enc_weight: bfloat16 [2, 3584, 8192], P('layer', 'token', 'latent'), may hold values from -0.0625 to 0.0625
- enc_bias: float32 [8192], P('latent'), may hold values from -3 to 3
- dec_weight: bfloat16 [2, 3584, 8192], P('layer', 'token', 'latent'), as said below
- dec_bias: float32 [2, 3584], P('layer'), may hold values from -3 to 3
Outputs:
- enc_grad: bfloat16 [2, 3584, 8192], P('layer', 'token', 'latent')
- dec_grad: bfloat16 [2, 3584, 8192], P('layer', 'token', 'latent')
Inputs may be any that keep to these rules, and one draw needn't show every extreme that they name: `token_ids`: id 2 marks the beginning of a document and stands at position 0; all other ids are 3 or more. `dec_weight`: entries of order 8192^-0.5.
All inputs are finite; a program needn't handle non-finite values.
Results may differ from a plain program's by a relative error of at most 0.014.
Values may be sent and summed in bfloat16 or wider, within the bound.
A program may use at most 64 MiB of HBM per device.

v0:
```python
import math

import jax
import jax.numpy as jnp
from jax import lax
from jax.sharding import PartitionSpec as P

KNEE_WIDTH = 0.5
SPARSITY = 0.5
BEGIN_TOKEN = 2


def smooth_relu(preact):
    positive = jnp.maximum(preact, 0.0)
    return jnp.where(
        positive < KNEE_WIDTH, positive * positive / (2.0 * KNEE_WIDTH), positive - 0.5 * KNEE_WIDTH
    )


def relu_slope(preact):
    return jnp.clip(preact / KNEE_WIDTH, 0.0, 1.0)


def local(taps, token_ids, enc_weight, enc_bias, dec_weight, dec_bias):
    tap_rows = taps[0]
    tokens_dev = tap_rows.shape[0]
    loss_scale = 1.0 / math.sqrt(tokens_dev * lax.axis_size("token"))
    keep_mask = (token_ids != BEGIN_TOKEN).astype(jnp.float32)
    partial_pre = jnp.dot(
        tap_rows,
        lax.all_gather(enc_weight[0], "token", axis=0, tiled=True),
        preferred_element_type=jnp.float32,
    )
    preact = lax.psum(partial_pre, "layer") + enc_bias[None, :]
    features = smooth_relu(preact).astype(jnp.bfloat16)
    dec_full = lax.all_gather(dec_weight[0], "token", axis=0, tiled=True)
    rebuilt_part = lax.dot_general(
        features, dec_full, (((1,), (1,)), ((), ())), preferred_element_type=jnp.float32
    )
    rebuilt = lax.psum(rebuilt_part, "latent") + dec_bias[0][None, :]
    residue = (loss_scale * keep_mask[:, None] * (rebuilt - tap_rows.astype(jnp.float32))).astype(
        jnp.bfloat16
    )
    colnorm = jnp.sqrt(jnp.sum(jnp.square(dec_full.astype(jnp.float32)), axis=0) + 1e-06)
    back_part = jnp.dot(residue, dec_full, preferred_element_type=jnp.float32)
    feat_back, norm_total = lax.psum((back_part, colnorm), "layer")
    feat_grads = feat_back + loss_scale * SPARSITY * keep_mask[:, None] * norm_total[None, :]
    pre_grads = (feat_grads * relu_slope(preact)).astype(jnp.bfloat16)
    activity = jnp.sum(keep_mask[:, None] * features.astype(jnp.float32), axis=0)
    penalty_scale = loss_scale * SPARSITY * activity / colnorm
    product = lax.dot_general(
        residue, features, (((0,), (0,)), ((), ())), preferred_element_type=jnp.float32
    )
    dec_grad = lax.psum_scatter(
        (product + dec_full.astype(jnp.float32) * penalty_scale[None, :]).astype(jnp.bfloat16),
        "token",
        scatter_dimension=0,
        tiled=True,
    )
    enc_grad = lax.psum_scatter(
        lax.dot_general(
            tap_rows, pre_grads, (((0,), (0,)), ((), ())), preferred_element_type=jnp.float32
        ).astype(jnp.bfloat16),
        "token",
        scatter_dimension=0,
        tiled=True,
    )
    return (enc_grad[None], dec_grad[None])


def solution(mesh):
    placed = (
        P("layer", "token", None),
        P("token"),
        P("layer", "token", "latent"),
        P("latent"),
        P("layer", "token", "latent"),
        P("layer", None),
    )
    return jax.shard_map(
        local,
        mesh=mesh,
        in_specs=placed,
        out_specs=(P("layer", "token", "latent"), P("layer", "token", "latent")),
        check_vma=False,
    )
```

profile of v0, /device:TPU:1, one launch (start us, length us, event | category | flops | bytes accessed | tf_op | source)
XLA Modules:
  0.0 1118.2 jit_solution(13959128137853227899)
XLA Ops:
  7.2 0.0 all-gather.5.cloned.1.call-start
  7.2 0.7 all-gather.5.cloned.1.call-update
  7.9 0.0 copy-start.6
  7.9 0.0 copy-start.7
  7.9 0.0 all-reduce.4.cloned.1.call-start
  8.0 72.1 %all-gather.5.cloned.1.call-done = bf16[1,3584,256]{2,1,0:T(8,128)(2,1)} async-done(((bf16[1,448,256]{2,1,0:T(8,128)(2,1)}), bf16[1,3584,256]{2,1,0:T(8,128)(2,1)}) %all-gather.5.cloned.1.call-update) | async-done | bytes 1835024 | tf_op jit(solution)/shard_map/all_gather | solution.py:31
  80.1 3.3 fusion.7
  83.4 0.0 all-reduce.4.cloned.1.call-update
  83.4 0.0 all-gather.7.cloned.1.call-start
  83.4 0.7 all-gather.7.cloned.1.call-update
  84.1 0.0 all-reduce.6.cloned.1.call-start
  84.2 0.0 copy-done.6
  84.2 41.0 %all-reduce.4.cloned.1.call-done = f32[224,256]{1,0:T(8,128)} async-done(((f32[224,256]{1,0:T(8,128)}), f32[224,256]{1,0:T(8,128)}) %all-reduce.4.cloned.1.call-update) | async-done | bytes 229392 | tf_op jit(solution)/shard_map/psum | solution.py:34
  125.2 0.0 copy-done.7
  125.2 1.6 multiply_reduce_fusion
  126.8 65.1 %all-gather.7.cloned.1.call-done = bf16[1,3584,256]{2,1,0:T(8,128)(2,1)} async-done(((bf16[1,448,256]{2,1,0:T(8,128)(2,1)}), bf16[1,3584,256]{2,1,0:T(8,128)(2,1)}) %all-gather.7.cloned.1.call-update) | async-done | bytes 1835024 | tf_op jit(solution)/shard_map/all_gather | solution.py:36
  191.9 3.9 fusion.5
  195.8 0.0 copy-start.4
  195.8 0.0 copy-start.1
  195.8 0.0 all-reduce.6.cloned.1.call-update
  195.9 0.0 all-reduce.8.cloned.1.call-start
  195.9 0.6 copy-done.4
  196.6 0.6 reduce
  197.2 0.6 broadcast_select_fusion
  197.8 691.9 %all-reduce.6.cloned.1.call-done = f32[224,3584]{1,0:T(8,128)} async-done(((f32[224,3584]{1,0:T(8,128)}), f32[224,3584]{1,0:T(8,128)}) %all-reduce.6.cloned.1.call-update) | async-done | bytes 3211280 | tf_op jit(solution)/shard_map/psum | solution.py:40
  889.7 0.0 copy-done.1
  889.7 0.0 copy-start
  889.7 2.6 multiply_convert_fusion
  892.3 0.0 copy-start.2
  892.3 1.2 copy-done.2
  893.4 0.0 copy-done
  893.4 1.3 fusion.3
  894.7 0.0 all-reduce.8.cloned.1.call-update
  894.7 0.0 reduce-scatter.7.cloned.1.call-start
  894.8 0.0 copy-start.5
  894.8 0.5 fusion.2
  895.3 0.2 copy-done.5
  895.5 0.6 rsqrt_multiply_fusion
  896.0 23.9 %psum.31 = f32[256]{0:T(256)} all-reduce(f32[256]{0:T(256)} %get-tuple-element.9), channel_id=1, replica_groups=mesh['layer'=2,'latent'=32,'token'=8] {'layer'}, use_global_device_ids=true, to_apply=%region_4.5 | all-reduce | flops 256 | bytes 2048 | tf_op jit(solution)/shard_map/psum | solution.py:46
  919.9 47.6 %all-reduce.8.cloned.1.call-done = f32[224,256]{1,0:T(8,128)} async-done(((f32[224,256]{1,0:T(8,128)}), f32[224,256]{1,0:T(8,128)}) %all-reduce.8.cloned.1.call-update) | async-done | bytes 229392 | tf_op jit(solution)/shard_map/psum | solution.py:46
  967.5 3.0 fusion.1
  970.6 3.8 copy.10
  974.4 0.0 copy-start.3
  974.4 0.0 reduce-scatter.7.cloned.1.call-update
  974.4 0.0 reduce-scatter.5.cloned.1.call-start
  974.5 1.3 copy-done.3
  975.8 2.6 fusion
  978.4 0.0 reduce-scatter.5.cloned.1.call-update
  978.5 62.3 %reduce-scatter.7.cloned.1.call-done = bf16[448,256]{1,0:T(8,128)(2,1)} async-done(((bf16[3584,256]{1,0:T(8,128)(2,1)}), bf16[448,256]{1,0:T(8,128)(2,1)}) %reduce-scatter.7.cloned.1.call-update) | async-done | bytes 229392
  1040.8 1.1 copy.11
  1041.8 0.8 copy.9
  1042.7 68.7 %reduce-scatter.5.cloned.1.call-done = bf16[448,256]{1,0:T(8,128)(2,1)} async-done(((bf16[3584,256]{1,0:T(8,128)(2,1)}), bf16[448,256]{1,0:T(8,128)(2,1)}) %reduce-scatter.5.cloned.1.call-update) | async-done | bytes 229392 | tf_op jit(solution)/shard_map/reduce_scatter | solution.py:54
  (1 shorter events, 0.0 us)
Async XLA Ops:
  7.2 72.9 %all-gather.5.cloned.1.call-start = ((), (), s32[]{:S(2)}) async-start(), calls=%async_computation.6 | async-start | bytes 2064384 | tf_op jit(solution)/shard_map/all_gather | solution.py:31
  7.9 76.3 %copy-start.6 = (s32[224]{0:T(256)S(1)}, s32[224]{0:T(256)}, u32[]{:S(2)}) copy-start(s32[224]{0:T(256)} %param.7) | copy-start | bytes 2692
  7.9 117.3 %copy-start.7 = (f32[256]{0:T(256)S(1)}, f32[256]{0:T(256)}, u32[]{:S(2)}) copy-start(f32[256]{0:T(256)} %param.9) | copy-start | bytes 3076
  7.9 117.3 %all-reduce.4.cloned.1.call-start = ((), (), s32[]{:S(2)}) async-start(), calls=%async_computation.2 | async-start | bytes 458752 | tf_op jit(solution)/shard_map/psum | solution.py:34
  83.4 108.5 %all-gather.7.cloned.1.call-start = ((), (), s32[]{:S(2)}) async-start(), calls=%async_computation.7 | async-start | bytes 2064384 | tf_op jit(solution)/shard_map/all_gather | solution.py:36
  84.1 805.6 %all-reduce.6.cloned.1.call-start = ((), (), s32[]{:S(2)}) async-start(), calls=%async_computation.3 | async-start | bytes 6422528 | tf_op jit(solution)/shard_map/psum | solution.py:40
  195.8 0.7 copy-start.4
  195.8 693.8 %copy-start.1 = (bf16[1,224,3584]{2,1,0:T(8,128)(2,1)S(1)}, bf16[1,224,3584]{2,1,0:T(8,128)(2,1)}, u32[]{:S(2)}) copy-start(bf16[1,224,3584]{2,1,0:T(8,128)(2,1)} %param.6) | copy-start | bytes 4816900
  195.9 771.7 %all-reduce.8.cloned.1.call-start = ((), (), s32[]{:S(2)}) async-start(), calls=%async_computation.4 | async-start | bytes 458752 | tf_op jit(solution)/shard_map/psum | solution.py:46
  889.7 3.7 copy-start
  892.3 1.2 copy-start.2
  894.7 146.0 %reduce-scatter.7.cloned.1.call-start = ((), (), s32[]{:S(2)}) async-start(), calls=%async_computation.8 | async-start | bytes 2064384
  894.8 0.7 copy-start.5
  974.4 1.4 copy-start.3
  974.4 137.0 %reduce-scatter.5.cloned.1.call-start = ((), (), s32[]{:S(2)}) async-start(), calls=%async_computation.5 | async-start | bytes 2064384 | tf_op jit(solution)/shard_map/reduce_scatter | solution.py:54
Sparse Core Ops, SparseCore 0:
  10.1 69.9 all-gather.4
  83.6 41.6 all-reduce.3
  127.3 64.5 all-gather.6
  196.0 693.6 all-reduce.5
  894.9 72.6 all-reduce.7
  974.5 66.1 reduce-scatter.6
  1044.4 66.9 reduce-scatter.4
where the time goes:
time: 1120 us
  waiting for transfers between devices  1050 us (94%)
  blocking collectives  23.9 us (2%)
  between operations  14.2 us (1%)
  matrix products  14.1 us (1%)
    psum x1, waiting for transfers between devices, local(): rebuilt = lax.psum(rebuilt_part, 'latent') + dec_bias[0][None, :]  692 us
    all_gather x1, waiting for transfers between devices, local(): lax.all_gather(enc_weight[0], 'token', axis=0, tiled=True)  72.1 us
    reduce_scatter x1, waiting for transfers between devices, local(): lax.psum_scatter((product + dec_full.astype(jnp.float32) * penalty_scale[...  68.7 us
    all_gather x1, waiting for transfers between devices, local(): dec_full = lax.all_gather(dec_weight[0], 'token', axis=0, tiled=True)  65.1 us
    unnamed x8, waiting for transfers between devices  63.7 us
    psum x1, waiting for transfers between devices, local(): feat_back, norm_total = lax.psum((back_part, colnorm), 'layer')  47.6 us
    psum x1, waiting for transfers between devices, local(): preact = lax.psum(partial_pre, 'layer') + enc_bias[None, :]  41 us
    psum x1, blocking collectives, local(): feat_back, norm_total = lax.psum((back_part, colnorm), 'layer')  23.9 us
  transfers between devices with their start and end apart: 7, of which 7 were waited for; matrix products, arithmetic and copies ran while one was open for 1% of the time, Pallas kernels for 0%

commit v1 on v0

v1 whole, which is shorter than its diff:
```python
import functools
import math

import jax
import jax.numpy as jnp
from jax import lax
from jax.experimental import pallas as pl
from jax.experimental.pallas import tpu as pltpu
from jax.sharding import PartitionSpec as P

KNEE_WIDTH = 0.5
SPARSITY = 0.5
BEGIN_TOKEN = 2
MESH = pl.DeviceIdType.MESH
F32 = jnp.float32
BF16 = jnp.bfloat16

CHUNKS = 2
ROWS = 112
TILES = 7
PAIR = 896
SHARES = 14


def smooth_relu(preact):
    positive = jnp.maximum(preact, 0.0)
    return jnp.where(
        positive < KNEE_WIDTH, positive * positive / (2.0 * KNEE_WIDTH), positive - 0.5 * KNEE_WIDTH
    )


def relu_slope(preact):
    return jnp.clip(preact / KNEE_WIDTH, 0.0, 1.0)


def kernel(loss_scale, taps, ids, we, eb, wd, db, enc_out, dec_out,
           x_t, w_e, w_d, mask, keep, nsq, cnorm, cnorm_o,
           pre_f, pre_x, pre_s, pre_r, pre_own, feat, reb, reb_r, zs, zb, zr, res,
           g_f, g_x, g_s, g_r, g_own, pg, dwd, dwd_s, dwd_r, dwe, dwe_s, dwe_r,
           loc, xz_s, xz_r, xy_s, xy_r, mk_s, mk_r, ns_s, ns_r, one_s, one_r,
           co_s, co_r, zg_s, zg_r, rr_s, rr_r, zh_s, zh_r, rs_s, rs_r):
    layer = lax.axis_index("layer")
    n = lax.axis_index("latent")
    m = lax.axis_index("token")
    h = n // 16
    y = (n // 4) % 4
    x = n % 4
    s = n % 16
    p = m // 2
    r = m % 2

    other_core = (1 - layer, n, m)
    twin = (layer, n, 2 * p + 1 - r)
    far = (layer, (1 - h) * 16 + s, m)

    def zpeer(k):
        return (layer, n, 2 * ((p + k) % 4) + r)

    def xy_to(k):
        return ((y + k // 4) % 4) * 4 + (x + k % 4) % 4

    def xy_from(k):
        return ((y + 4 - k // 4) % 4) * 4 + (x + 4 - k % 4) % 4

    def xypeer(k):
        return (layer, h * 16 + xy_to(k), m)

    def half(i):
        return pl.ds(pl.multiple_of(i * 128, 128), 128)

    mine, theirs = half(layer), half(1 - layer)
    cols = pl.ds(pl.multiple_of(p * PAIR, 128), PAIR)

    def share(i):
        return pl.ds((i // TILES) * 2, 2), pl.ds(pl.multiple_of((i % TILES) * 16, 16), 16)

    def remote(src, dst, send, recv, dev):
        return pltpu.make_async_remote_copy(
            src_ref=src, dst_ref=dst, send_sem=send, recv_sem=recv, device_id=dev, device_id_type=MESH
        )

    local = [
        pltpu.make_async_copy(taps.at[pl.ds(ROWS * c, ROWS), cols], x_t.at[c, 0], loc.at[c])
        for c in range(CHUNKS)
    ]
    local.append(pltpu.make_async_copy(we, w_e.at[r], loc.at[CHUNKS]))
    local.append(pltpu.make_async_copy(wd, w_d.at[r], loc.at[CHUNKS + 1]))
    for cp in local:
        cp.start()

    barrier = pltpu.get_barrier_semaphore()
    partners = [other_core, twin, far] + [zpeer(k) for k in (1, 2, 3)] + [xypeer(k) for k in range(1, 16)]
    for dev in partners:
        pl.semaphore_signal(barrier, inc=1, device_id=dev, device_id_type=MESH)
    keep_row = (ids[...] != BEGIN_TOKEN).astype(F32)
    mask[0] = jnp.broadcast_to(keep_row, mask.shape[1:]).astype(BF16)
    pl.semaphore_wait(barrier, len(partners))

    sends = []

    def go(cp):
        cp.start()
        sends.append(cp)
        return cp

    owns = s < SHARES

    s_in = lax.min(s, SHARES - 1)
    s_chunk, s_row = s_in // TILES, pl.ds(pl.multiple_of((s_in % TILES) * 16, 16), 16)
    s_src = pl.ds(pl.multiple_of(s_in * 16, 16), 16)

    def xz(k):
        there = pl.ds(pl.multiple_of(((p + k) % 4) * PAIR, 128), PAIR)
        return remote(taps.at[s_src, there], x_t.at[s_chunk, 4 - k, s_row], xz_s.at[k - 1], xz_r.at[3 - k], zpeer(k))

    def xz_here(k):
        return remote(taps.at[s_src, cols], x_t.at[s_chunk, 4 - k, s_row], xz_s.at[k - 1], xz_r.at[3 - k], zpeer(k))

    @pl.when(owns)
    def _():
        for k in (1, 2, 3):
            xz(k).start()

    we_cp = go(remote(we, w_e.at[r], one_s.at[0], one_r.at[0], twin))
    wd_cp = go(remote(wd, w_d.at[r], one_s.at[1], one_r.at[1], twin))
    mask_cp = [go(remote(mask.at[0], mask.at[4 - k], mk_s.at[k - 1], mk_r.at[3 - k], zpeer(k))) for k in (1, 2, 3)]

    def xy(k, row_chunk, row):
        part = x_t.at[row_chunk, pl.ds(1, 3), row]
        return remote(part, part, xy_s.at[k - 1], xy_r.at[k - 1], xypeer(k))

    @pl.when(owns)
    def _():
        for k in (1, 2, 3):
            xz_here(k).wait_recv()
        for k in range(1, 16):
            xy(k, s_chunk, s_row).start()

    for cp in local:
        cp.wait()
    wd_cp.wait_recv()
    w_sq = jnp.square(w_d[...].astype(F32)).reshape(PAIR, 256)
    nsq[0] = jnp.broadcast_to(jnp.sum(w_sq, axis=0, keepdims=True), (8, 256))
    ns_cp = [go(remote(nsq.at[0], nsq.at[4 - k], ns_s.at[k - 1], ns_r.at[3 - k], zpeer(k))) for k in (1, 2, 3)]
    for cp in mask_cp:
        cp.wait_recv()
    unit = jnp.full((16, 128), 1.0 / 16.0, BF16)
    for q in range(4):
        column = lax.dot_general(mask[q], unit, (((0,), (0,)), ((), ())), preferred_element_type=F32)
        for c in range(CHUNKS):
            keep[c, q] = column[c * ROWS:(c + 1) * ROWS]
    for cp in ns_cp:
        cp.wait_recv()
    cnorm[...] = jnp.sqrt(nsq[0] + nsq[1] + nsq[2] + nsq[3] + 1e-06)
    cn_cp = go(remote(cnorm, cnorm_o, one_s.at[2], one_r.at[2], other_core))
    we_cp.wait_recv()

    for k in range(1, 16):
        source = xy_from(k)

        @pl.when(source < SHARES)
        def _():
            there = lax.min(source, SHARES - 1)
            row = pl.ds(pl.multiple_of((there % TILES) * 16, 16), 16)
            xy(k, there // TILES, row).wait_recv()

    def z_group(sem, src, dst, c):
        return [
            go(remote(src(k), dst(4 - k), zg_s.at[sem, c, k - 1], zg_r.at[sem, c, 3 - k], zpeer(k)))
            for k in (1, 2, 3)
        ]

    enc = w_e[...].reshape(PAIR, 256)
    dec = w_d[...].reshape(PAIR, 256)

    def cross(c, sem, full, got):
        return go(remote(full.at[c, :, :, theirs], got.at[c], co_s.at[sem, c], co_r.at[sem, c], other_core))

    step = {}
    for c in range(CHUNKS):
        part = jnp.dot(x_t[c].reshape(4 * ROWS, PAIR), enc, preferred_element_type=F32)
        pre_f[c] = part.reshape(4, ROWS, 256)
        step["pc", c] = cross(c, 0, pre_f, pre_x)
    for c in range(CHUNKS):
        step["pc", c].wait_recv()
        pre_own[c] = pre_f[c, 0, :, mine] + pre_x[c, 0]
        for q in (1, 2, 3):
            pre_s[c, q - 1] = (pre_f[c, q, :, mine] + pre_x[c, q]).astype(BF16)
        step["pz", c] = z_group(0, lambda k: pre_s.at[c, k - 1], lambda q: pre_r.at[c, q - 1], c)
    for c in range(CHUNKS):
        for cp in step["pz", c]:
            cp.wait_recv()
        preact = pre_own[c] + eb[:, mine]
        for q in range(3):
            preact = preact + pre_r[c, q].astype(F32)
        pre_own[c] = preact
        feat[c, 0, :, mine] = smooth_relu(preact).astype(BF16)
        step["fz", c] = z_group(1, lambda k: feat.at[c, 0, :, mine], lambda q: feat.at[c, q, :, mine], c)
    for c in range(CHUNKS):
        for cp in step["fz", c]:
            cp.wait_recv()
        block = feat.at[c, :, :, mine]
        step["fc", c] = go(remote(block, block, co_s.at[1, c], co_r.at[1, c], other_core))

    def rr(c, k):
        blocks, row = share(lax.min(xy_to(k), SHARES - 1))
        return remote(reb.at[c, blocks, row], reb_r.at[c, k - 1], rr_s.at[c, k - 1], rr_r.at[c, k - 1], xypeer(k))

    blocks, row = share(s_in)

    def rs(c, k, blocks, row):
        part = res.at[c, blocks, row]
        return remote(part, part, rs_s.at[c, k - 1], rs_r.at[c, k - 1], xypeer(k))

    def zh(c):
        return remote(zb.at[c], zr.at[c], zh_s.at[c], zh_r.at[c], far)

    for c in range(CHUNKS):
        step["fc", c].wait_recv()
        part = lax.dot_general(
            feat[c].reshape(4 * ROWS, 256), dec, (((1,), (1,)), ((), ())), preferred_element_type=F32
        )
        reb[c] = part.astype(BF16).reshape(4, ROWS, PAIR)
        for k in range(1, 16):

            @pl.when(xy_to(k) < SHARES)
            def _():
                rr(c, k).start()

    for c in range(CHUNKS):

        @pl.when(owns)
        def _():
            total = reb[c, blocks, row].astype(F32)
            for k in range(1, 16):
                rr(c, k).wait_recv()
                total = total + reb_r[c, k - 1].astype(F32)
            zs[c] = total
            zb[c] = total.astype(BF16)
            zh(c).start()

    for c in range(CHUNKS):

        @pl.when(owns)
        def _():
            zh(c).wait_recv()
            rebuilt = zs[c] + zr[c].astype(F32) + db[:, cols].reshape(1, 1, PAIR)
            diff = rebuilt - x_t[c, blocks, row].astype(F32)
            weight = loss_scale * keep[c, blocks, row][:, :, :1]
            res[c, blocks, row] = (weight * diff).astype(BF16)
            for k in range(1, 16):
                rs(c, k, blocks, row).start()

    for c in range(CHUNKS):
        for k in range(1, 16):
            source = xy_from(k)

            @pl.when(source < SHARES)
            def _():
                rs(c, k, *share(lax.min(source, SHARES - 1))).wait_recv()

        part = jnp.dot(res[c].reshape(4 * ROWS, PAIR), dec, preferred_element_type=F32)
        g_f[c] = part.reshape(4, ROWS, 256)
        step["gc", c] = cross(c, 2, g_f, g_x)
    cn_cp.wait_recv()
    for c in range(CHUNKS):
        step["gc", c].wait_recv()
        g_own[c] = g_f[c, 0, :, mine] + g_x[c, 0]
        for q in (1, 2, 3):
            g_s[c, q - 1] = (g_f[c, q, :, mine] + g_x[c, q]).astype(BF16)
        step["gz", c] = z_group(2, lambda k: g_s.at[c, k - 1], lambda q: g_r.at[c, q - 1], c)
    norm_total = cnorm[0:1, mine] + cnorm_o[0:1, mine]
    for c in range(CHUNKS):
        for cp in step["gz", c]:
            cp.wait_recv()
        grads = g_own[c] + loss_scale * SPARSITY * keep[c, 0] * norm_total
        for q in range(3):
            grads = grads + g_r[c, q].astype(F32)
        pg[c, 0, :, mine] = (grads * relu_slope(pre_own[c])).astype(BF16)
        step["qz", c] = z_group(3, lambda k: pg.at[c, 0, :, mine], lambda q: pg.at[c, q, :, mine], c)

    activity = jnp.zeros((1, 256), F32)
    for c in range(CHUNKS):
        f = feat[c].reshape(4 * ROWS, 256)
        k_col = keep[c].reshape(4 * ROWS, 128)[:, :1]
        activity = activity + jnp.sum(k_col * f.astype(F32), axis=0, keepdims=True)
    penalty = loss_scale * SPARSITY * activity / cnorm[0:1, :]
    total = dec.astype(F32) * penalty
    for c in range(CHUNKS):
        total = total + lax.dot_general(
            res[c].reshape(4 * ROWS, PAIR), feat[c].reshape(4 * ROWS, 256), (((0,), (0,)), ((), ())),
            preferred_element_type=F32,
        )
    dwd[...] = total.reshape(2, PAIR // 2, 256)
    dwd_s[...] = dwd[1 - r].astype(BF16)
    dwd_cp = go(remote(dwd_s, dwd_r, one_s.at[3], one_r.at[3], twin))

    for c in range(CHUNKS):
        for cp in step["qz", c]:
            cp.wait_recv()
        block = pg.at[c, :, :, mine]
        step["qc", c] = go(remote(block, block, co_s.at[3, c], co_r.at[3, c], other_core))
    total = jnp.zeros((PAIR, 256), F32)
    for c in range(CHUNKS):
        step["qc", c].wait_recv()
        total = total + lax.dot_general(
            x_t[c].reshape(4 * ROWS, PAIR), pg[c].reshape(4 * ROWS, 256), (((0,), (0,)), ((), ())),
            preferred_element_type=F32,
        )
    dwe[...] = total.reshape(2, PAIR // 2, 256)
    dwe_s[...] = dwe[1 - r].astype(BF16)
    dwe_cp = go(remote(dwe_s, dwe_r, one_s.at[4], one_r.at[4], twin))
    dwd_cp.wait_recv()
    dec_out[...] = (dwd[r] + dwd_r[...].astype(F32)).astype(BF16)
    dwe_cp.wait_recv()
    enc_out[...] = (dwe[r] + dwe_r[...].astype(F32)).astype(BF16)

    for cp in sends:
        cp.wait_send()

    @pl.when(owns)
    def _():
        for k in (1, 2, 3):
            xz(k).wait_send()
        for k in range(1, 16):
            xy(k, s_chunk, s_row).wait_send()
        for c in range(CHUNKS):
            zh(c).wait_send()
            for k in range(1, 16):
                rs(c, k, blocks, row).wait_send()

    for c in range(CHUNKS):
        for k in range(1, 16):

            @pl.when(xy_to(k) < SHARES)
            def _():
                rr(c, k).wait_send()


def local(taps, token_ids, enc_weight, enc_bias, dec_weight, dec_bias):
    tokens_dev = taps.shape[1]
    loss_scale = 1.0 / math.sqrt(tokens_dev * lax.axis_size("token"))
    c = CHUNKS
    dma = pltpu.SemaphoreType.DMA
    vmem = pltpu.VMEM
    scratch = [
        vmem((c, 4, ROWS, PAIR), BF16),
        vmem((2, 448, 256), BF16), vmem((2, 448, 256), BF16),
        vmem((4, 16, 224), BF16), vmem((c, 4, ROWS, 128), F32),
        vmem((4, 8, 256), F32), vmem((8, 256), F32), vmem((8, 256), F32),
        vmem((c, 4, ROWS, 256), F32), vmem((c, 4, ROWS, 128), F32),
        vmem((c, 3, ROWS, 128), BF16), vmem((c, 3, ROWS, 128), BF16), vmem((c, ROWS, 128), F32),
        vmem((c, 4, ROWS, 256), BF16),
        vmem((c, 4, ROWS, PAIR), BF16), vmem((c, 15, 2, 16, PAIR), BF16),
        vmem((c, 2, 16, PAIR), F32), vmem((c, 2, 16, PAIR), BF16), vmem((c, 2, 16, PAIR), BF16),
        vmem((c, 4, ROWS, PAIR), BF16),
        vmem((c, 4, ROWS, 256), F32), vmem((c, 4, ROWS, 128), F32),
        vmem((c, 3, ROWS, 128), BF16), vmem((c, 3, ROWS, 128), BF16), vmem((c, ROWS, 128), F32),
        vmem((c, 4, ROWS, 256), BF16),
        vmem((2, 448, 256), F32), vmem((448, 256), BF16), vmem((448, 256), BF16),
        vmem((2, 448, 256), F32), vmem((448, 256), BF16), vmem((448, 256), BF16),
        dma((c + 2,)),
        dma((3,)), dma((3,)), dma((15,)), dma((15,)), dma((3,)), dma((3,)), dma((3,)), dma((3,)),
        dma((5,)), dma((5,)),
        dma((4, c)), dma((4, c)), dma((4, c, 3)), dma((4, c, 3)),
        dma((c, 15)), dma((c, 15)), dma((c,)), dma((c,)), dma((c, 15)), dma((c, 15)),
    ]
    any_spec = pl.BlockSpec(memory_space=pl.ANY)
    vmem_spec = pl.BlockSpec(memory_space=pltpu.VMEM)
    enc_grad, dec_grad = pl.pallas_call(
        functools.partial(kernel, loss_scale),
        out_shape=(jax.ShapeDtypeStruct((448, 256), BF16), jax.ShapeDtypeStruct((448, 256), BF16)),
        in_specs=[any_spec, vmem_spec, any_spec, vmem_spec, any_spec, vmem_spec],
        out_specs=(vmem_spec, vmem_spec),
        scratch_shapes=scratch,
        compiler_params=pltpu.CompilerParams(
            collective_id=0, has_side_effects=True, vmem_limit_bytes=40 * 1024 * 1024
        ),
        name="crosscoder",
    )(taps[0], token_ids[None, :], enc_weight[0], enc_bias[None, :], dec_weight[0], dec_bias)
    return enc_grad[None], dec_grad[None]


def solution(mesh):
    placed = (
        P("layer", "token", None),
        P("token"),
        P("layer", "token", "latent"),
        P("latent"),
        P("layer", "token", "latent"),
        P("layer", None),
    )
    return jax.shard_map(
        local,
        mesh=mesh,
        in_specs=placed,
        out_specs=(P("layer", "token", "latent"), P("layer", "token", "latent")),
        check_vma=False,
    )
```

time: 1120 us -> 154 us (0.14)
  waiting for transfers between devices: 1050 us -> 0 us
  Pallas kernels: 0 us -> 146 us
  blocking collectives: 23.9 us -> 0 us
  matrix products: 14.1 us -> 0 us
  between operations: 14.2 us -> 0.65 us
    psum x3 -> x0, waiting for transfers between devices: 781 us -> none  [the longest x1 692 us: local(): rebuilt = lax.psum(rebuilt_part, 'latent') + dec_bias[0][None, :]]
    pallas_call x0 -> x1, Pallas kernels: none -> 146 us  [local(): pl.pallas_call(functools.partial(kernel, loss_scale), out_shape=(jax.Shap...]
    all_gather x2 -> x0, waiting for transfers between devices: 137 us -> none  [the longest x1 72.1 us: local(): lax.all_gather(enc_weight[0], 'token', axis=0, tiled=True)]
    reduce_scatter x1 -> x0, waiting for transfers between devices: 68.7 us -> none  [local(): lax.psum_scatter((product + dec_full.astype(jnp.float32) * penalty_scale[...]
    unnamed x8 -> x0, waiting for transfers between devices: 63.7 us -> none
    psum x1 -> x0, blocking collectives: 23.9 us -> none  [local(): feat_back, norm_total = lax.psum((back_part, colnorm), 'layer')]
    dot_general x5 -> x0, matrix products: 14.1 us -> none  [the longest x1 3.92 us: local(): lax.dot_general(features, dec_full, (((1,), (1,)), ((), ())), preferred_e...]
  transfers between devices with their start and end apart: 7 -> 0, of which waited for: 7 -> 0; matrix products, arithmetic and copies ran while one was open for 1% -> 0% of each run, Pallas kernels for 0% -> 0%
where the time goes in v1:
time: 154 us
  Pallas kernels  146 us (95%)
  local copies, waits for them, and re-layouts  6.73 us (4%)
    pallas_call x1, Pallas kernels, local(): pl.pallas_call(functools.partial(kernel, loss_scale), out_shape=(jax.Shap...  146 us
    unnamed x14, local copies, waits for them, and re-layouts  6.73 us

profile of v1, /device:TPU:1, one launch (start us, length us, event | category | flops | bytes accessed | tf_op | source)
XLA Modules:
  0.0 153.8 jit_solution(11169076601842494713)
XLA Ops:
  0.6 0.0 copy-start
  0.6 1.4 copy-done
  2.1 0.0 copy-start.1
  2.1 0.9 copy-done.1
  3.0 0.0 copy-start.2
  3.0 0.9 copy-done.2
  3.9 0.0 copy-start.3
  3.9 0.7 copy-done.3
  4.6 0.0 copy-start.4
  4.6 0.7 copy-done.4
  5.3 0.0 copy-start.5
  5.3 0.7 copy-done.5
  6.0 146.4 %crosscoder.1 = (bf16[448,256]{1,0:T(8,128)(2,1)S(1)}, bf16[448,256]{1,0:T(8,128)(2,1)S(1)}) custom-call(bf16[224,3584]{1,0:T(8,128)(2,1)S(1)} %bitcast.7, s32[1,224]{1,0:T(1,128)S(1)} %bitcast.12, bf16[448,256]{1,0:T(8,128)(2,1)S(1)} %bitcast.10, f32[1,256]{1,0:T(1,128)S(1)} %bitcast.13, bf16[448,256]{1,0:T(8,128)(2,1)S(1)} %bitcast.11, f32[1,3584]{1,0:T(1,128)S(1)} %copy-done.3), custom_call_target="tpu_custom_call" | custom-call | tf_op jit(solution)/shard_map/crosscoder/pallas_call | solution.py:370
  152.4 0.7 copy.10
  153.1 0.7 copy.11
Async XLA Ops:
  0.6 1.4 copy-start
  2.1 0.9 copy-start.1
  3.0 0.9 copy-start.2
  3.9 0.7 copy-start.3
  4.6 0.7 copy-start.4
  5.3 0.7 copy-start.5

commit v2 on v0

v2 whole, which is shorter than its diff:
```python
import functools
import math

import jax
import jax.numpy as jnp
from jax import lax
from jax.experimental import pallas as pl
from jax.experimental.pallas import tpu as pltpu
from jax.sharding import PartitionSpec as P

KNEE_WIDTH = 0.5
SPARSITY = 0.5
BEGIN_TOKEN = 2
MESH = pl.DeviceIdType.MESH
F32 = jnp.float32
BF16 = jnp.bfloat16

CHUNKS = 2
ROWS = 112
PADDED = 128
TILES = 7
PAIR = 896

CHAIN = (
    "taps_first", "taps_second", "pre_dot", "pre_sum", "pre_act", "feat_cross", "reb_dot", "reb_mid", "reb_sum",
    "residue", "residue_second", "grad_dot", "grad_sum", "dec_grad", "grad_pre", "grad_cross", "enc_grad",
)
LAG = 1
ORDER = [
    (stage, c) for _, c, stage in sorted((i + LAG * c, c, s) for i, s in enumerate(CHAIN) for c in range(CHUNKS))
]
ORDER.insert(ORDER.index(("pre_sum", CHUNKS - 1)) + 1, ("norms_first", 0))
ORDER.insert(ORDER.index(("reb_dot", 0)) + 1, ("norms_second", 0))


def smooth_relu(preact):
    positive = jnp.maximum(preact, 0.0)
    return jnp.where(
        positive < KNEE_WIDTH, positive * positive / (2.0 * KNEE_WIDTH), positive - 0.5 * KNEE_WIDTH
    )


def relu_slope(preact):
    return jnp.clip(preact / KNEE_WIDTH, 0.0, 1.0)


def kernel(loss_scale, taps, ids_in, we, eb, wd, db, enc_out, dec_out,
           ids, bias, dbias, x_t, w_e, w_d, mask, keep, nsq, cnorm, cnorm_o,
           pre_f, pre_x, pre_s, pre_r, pre_own, feat, reb, row_r, col_r, row_s, col_s, own_s, end_r,
           zs, zb, zr, res, g_f, g_x, g_s, g_r, g_own, pg, dwd, dwd_s, dwd_r, dwe, dwe_s, dwe_r,
           loc, xz_s, xz_r, xy_s, xy_r, mk_s, mk_r, ns_s, ns_r, one_s, one_r,
           co_s, co_r, zg_s, zg_r, rr_s, rr_r, zh_s, zh_r, rs_s, rs_r):
    layer = lax.axis_index("layer")
    n = lax.axis_index("latent")
    m = lax.axis_index("token")
    h = n // 16
    y = (n // 4) % 4
    x = n % 4
    p = m // 2
    r = m % 2

    other_core = (1 - layer, n, m)
    twin = (layer, n, 2 * p + 1 - r)
    far = (layer, (1 - h) * 16 + n % 16, m)

    def zpeer(k):
        return (layer, n, 2 * ((p + k) % 4) + r)

    def chip(yy, xx):
        return (layer, h * 16 + yy * 4 + xx, m)

    def half(i):
        return pl.ds(pl.multiple_of(i * 128, 128), 128)

    mine, theirs = half(layer), half(1 - layer)
    cols = pl.ds(pl.multiple_of(p * PAIR, 128), PAIR)
    real = pl.ds(0, ROWS)

    def has_tile(yy, xx):
        return jnp.logical_not(jnp.logical_and(yy % 2 == 1, xx == 3))

    owns = has_tile(y, x)

    def remote(src, dst, send, recv, dev):
        return pltpu.make_async_remote_copy(
            src_ref=src, dst_ref=dst, send_sem=send, recv_sem=recv, device_id=dev, device_id_type=MESH
        )

    local = []
    for c in range(CHUNKS):
        local.append(pltpu.make_async_copy(taps.at[pl.ds(TILES * c, 4), :, cols], x_t.at[c, 0, 0, 0], loc.at[2 * c]))
        local.append(
            pltpu.make_async_copy(
                taps.at[pl.ds(TILES * c + 4, 3), :, cols], x_t.at[c, 0, 0, 1, pl.ds(0, 3)], loc.at[2 * c + 1]
            )
        )
    ids_cp = pltpu.make_async_copy(ids_in, ids, loc.at[2 * CHUNKS])
    ids_cp.start()
    local.append(pltpu.make_async_copy(eb.at[:, mine], bias, loc.at[2 * CHUNKS + 1]))
    local.append(pltpu.make_async_copy(db.at[:, cols], dbias, loc.at[2 * CHUNKS + 2]))
    local.append(pltpu.make_async_copy(we, w_e.at[r], loc.at[2 * CHUNKS + 3]))
    local.append(pltpu.make_async_copy(wd, w_d.at[r], loc.at[2 * CHUNKS + 4]))
    for cp in local:
        cp.start()

    for c in range(CHUNKS):
        for q in range(4):
            x_t[c, q // 2, q % 2, 1, 3] = jnp.zeros((16, PAIR), BF16)
            res[c, q // 2, q % 2, 1, 3] = jnp.zeros((16, PAIR), BF16)
    barrier = pltpu.get_barrier_semaphore()
    partners = [far, other_core, twin] + [zpeer(k) for k in (1, 2, 3)]
    partners += [chip((y + k) % 4, x) for k in (1, 2, 3)] + [chip(y, (x + k) % 4) for k in (1, 2, 3)]
    for dev in partners:
        pl.semaphore_signal(barrier, inc=1, device_id=dev, device_id_type=MESH)
    for c in range(CHUNKS):
        for q in range(4):
            feat[c, q, ROWS:] = jnp.zeros((16, 256), BF16)
            pg[c, q, ROWS:] = jnp.zeros((16, 256), BF16)
            keep[c, q, ROWS:] = jnp.zeros((16, 128), F32)
    ids_cp.wait()
    keep_row = (ids[...] != BEGIN_TOKEN).astype(F32)
    mask[0] = jnp.broadcast_to(keep_row, mask.shape[1:]).astype(BF16)
    for cp in local:
        cp.wait()
    pl.semaphore_wait(barrier, len(partners))

    sends, pending, step = [], {}, {}

    def under(when, action):
        if when is None:
            action()
        else:
            pl.when(when)(action)

    def go(cp, when=None, arrives=None):
        under(when, cp.start)
        sends.append((cp, when))
        pending[len(sends)] = (cp, arrives)
        return len(sends)

    def got(*entries):
        for entry in entries:
            cp, arrives = pending.pop(entry)
            under(arrives, cp.wait_recv)

    def finish():
        got(*list(pending))
        for cp, when in sends:
            under(when, cp.wait_send)

    def both(a, b):
        return b if a is None else jnp.logical_and(a, b)

    def spread_first(buf, c, send, recv, rows=None):
        out = []
        for k in (1, 2, 3):
            xx, yy = (x + k) % 4, (y + k) % 4
            for u, dev, source in (
                (0, chip(y, xx), has_tile(y, (x + 4 - k) % 4)),
                (1, chip(yy, x), has_tile((y + 4 - k) % 4, x)),
            ):
                part = buf.at[c, y // 2, u, y % 2, x]
                lead = rows if u == 0 else None
                out.append(
                    go(remote(part, part, send.at[0, c, u, k - 1], recv.at[0, c, u, k - 1], dev),
                       both(lead, owns), both(lead, source))
                )
        return out

    def spread_second(buf, c, send, recv, rows=None):
        out = []
        for k in (1, 2, 3):
            xx, yy = (x + k) % 4, (y + k) % 4
            part = buf.at[c, y // 2, 0, y % 2]
            out.append(
                go(remote(part, part, send.at[1, c, 0, k - 1], recv.at[1, c, 0, k - 1], chip(yy, x)),
                   rows, None if rows is None else (y + 4 - k) % 4 >= 2)
            )
            part = buf.at[c, pl.ds(0, 2), 1, pl.ds(0, 2), x]
            out.append(go(remote(part, part, send.at[1, c, 1, k - 1], recv.at[1, c, 1, k - 1], chip(y, xx))))
        return out

    low = y >= 2
    tile = 4 * (y % 2) + x
    for c in range(CHUNKS):
        entries = []
        for k in (1, 2, 3):
            q = 4 - k
            there = pl.ds(pl.multiple_of(((p + k) % 4) * PAIR, 128), PAIR)
            when = both(low if q >= 2 else jnp.logical_not(low), owns)
            src = taps.at[lax.min(TILES * c + tile, taps.shape[0] - 1), :, there]
            dst = x_t.at[c, q // 2, q % 2, y % 2, x]
            entries.append(go(remote(src, dst, xz_s.at[c, k - 1], xz_r.at[c, q - 1], zpeer(k)), when, when))
        step["xz", c] = entries
    mask_cp = [go(remote(mask.at[0], mask.at[4 - k], mk_s.at[k - 1], mk_r.at[3 - k], zpeer(k))) for k in (1, 2, 3)]

    def taps_first(c):
        got(*step["xz", c])
        step["xa", c] = spread_first(x_t, c, xy_s, xy_r, low)
        if c == CHUNKS - 1:
            step["we"] = go(remote(we, w_e.at[r], one_s.at[0], one_r.at[0], twin))
            step["wd"] = go(remote(wd, w_d.at[r], one_s.at[1], one_r.at[1], twin))

    def taps_second(c):
        got(*step["xa", c])
        step["xb", c] = spread_second(x_t, c, xy_s, xy_r, low)

    def norms_first(c):
        got(step["wd"])
        w_sq = jnp.square(w_d[...].astype(F32)).reshape(PAIR, 256)
        nsq[0] = jnp.broadcast_to(jnp.sum(w_sq, axis=0, keepdims=True), (8, 256))
        step["ns"] = [
            go(remote(nsq.at[0], nsq.at[4 - k], ns_s.at[k - 1], ns_r.at[3 - k], zpeer(k))) for k in (1, 2, 3)
        ]
        got(*mask_cp)
        unit = jnp.full((16, 128), 1.0 / 16.0, BF16)
        for q in range(4):
            column = lax.dot_general(mask[q], unit, (((0,), (0,)), ((), ())), preferred_element_type=F32)
            for c in range(CHUNKS):
                keep[c, q, :ROWS] = column[c * ROWS:(c + 1) * ROWS]

    def norms_second(c):
        got(*step["ns"])
        cnorm[...] = jnp.sqrt(nsq[0] + nsq[1] + nsq[2] + nsq[3] + 1e-06)
        step["cn"] = go(remote(cnorm, cnorm_o, one_s.at[2], one_r.at[2], other_core))

    def z_group(sem, src, dst, c):
        return [
            go(remote(src(k), dst(4 - k), zg_s.at[sem, c, k - 1], zg_r.at[sem, c, 3 - k], zpeer(k)))
            for k in (1, 2, 3)
        ]

    def cross(c, sem, full, got_ref):
        return go(
            remote(full.at[c, :, real, theirs], got_ref.at[c], co_s.at[sem, c], co_r.at[sem, c], other_core)
        )

    def cross_half(c, sem, full):
        block = full.at[c, :, real, mine]
        return go(remote(block, block, co_s.at[sem, c], co_r.at[sem, c], other_core))

    def rows_of(ref, c):
        return ref[c].reshape(4 * PADDED, ref.shape[-1])

    def pre_dot(c):
        got(*step["xb", c])
        if c == 0:
            got(step["we"])
        part = jnp.dot(rows_of(x_t, c), w_e[...].reshape(PAIR, 256), preferred_element_type=F32)
        pre_f[c] = part.reshape(4, PADDED, 256)
        step["pc", c] = cross(c, 0, pre_f, pre_x)

    def pre_sum(c):
        got(step["pc", c])
        for q in (1, 2, 3):
            pre_s[c, q - 1] = (pre_f[c, q, :ROWS, mine] + pre_x[c, q]).astype(BF16)
        step["pz", c] = z_group(0, lambda k: pre_s.at[c, k - 1], lambda q: pre_r.at[c, q - 1], c)
        pre_own[c] = pre_f[c, 0, :ROWS, mine] + pre_x[c, 0]

    def pre_act(c):
        got(*step["pz", c])
        preact = pre_own[c] + bias[...]
        for q in range(3):
            preact = preact + pre_r[c, q].astype(F32)
        pre_own[c] = preact
        feat[c, 0, :ROWS, mine] = smooth_relu(preact).astype(BF16)
        step["fz", c] = z_group(1, lambda k: feat.at[c, 0, real, mine], lambda q: feat.at[c, q, real, mine], c)

    def feat_cross(c):
        got(*step["fz", c])
        step["fc", c] = cross_half(c, 1, feat)

    def reb_dot(c):
        got(step["fc", c])
        part = lax.dot_general(
            rows_of(feat, c), w_d[...].reshape(PAIR, 256), (((1,), (1,)), ((), ())), preferred_element_type=F32
        )
        reb[c] = part.astype(BF16).reshape(2, 2, 2, 4, 16, PAIR)
        step["ra", c] = []
        for k in (1, 2, 3):
            xx, yy = (x + k) % 4, (y + k) % 4
            step["ra", c].append(go(remote(
                reb.at[c, pl.ds(0, 2), 0, pl.ds(0, 2), xx], row_r.at[c, k - 1],
                rr_s.at[0, c, 0, k - 1], rr_r.at[0, c, 0, k - 1], chip(y, xx))))
            step["ra", c].append(go(remote(
                reb.at[c, yy // 2, 1, yy % 2], col_r.at[c, k - 1],
                rr_s.at[0, c, 1, k - 1], rr_r.at[0, c, 1, k - 1], chip(yy, x))))

    def reb_mid(c):
        got(*step["ra", c])
        total = reb[c, :, 0, :, x].astype(F32)
        for k in range(3):
            total = total + row_r[c, k].astype(F32)
        row_s[c] = total.astype(BF16)
        own_s[c, 0] = row_s[c, y // 2, y % 2]
        total = reb[c, y // 2, 1, y % 2].astype(F32)
        for k in range(3):
            total = total + col_r[c, k].astype(F32)
        col_s[c] = total.astype(BF16)
        own_s[c, 1] = col_s[c, x]
        step["rb", c] = []
        for k in (1, 2, 3):
            xx, yy = (x + k) % 4, (y + k) % 4
            step["rb", c].append(go(remote(
                row_s.at[c, yy // 2, yy % 2], end_r.at[c, k - 1, 0],
                rr_s.at[1, c, 0, k - 1], rr_r.at[1, c, 0, k - 1], chip(yy, x)), has_tile(yy, x), owns))
            step["rb", c].append(go(remote(
                col_s.at[c, xx], end_r.at[c, k - 1, 1],
                rr_s.at[1, c, 1, k - 1], rr_r.at[1, c, 1, k - 1], chip(y, xx)), has_tile(y, xx), owns))

    def reb_sum(c):
        got(*step["rb", c])

        @pl.when(owns)
        def _():
            total = own_s[c].astype(F32)
            for k in range(3):
                total = total + end_r[c, k].astype(F32)
            zs[c] = total
            zb[c] = total.astype(BF16)

        step["zh", c] = go(remote(zb.at[c], zr.at[c], zh_s.at[c], zh_r.at[c], far), owns, owns)

    def residue(c):
        got(step["zh", c])

        @pl.when(owns)
        def _():
            rebuilt = zs[c] + zr[c].astype(F32) + dbias[...].reshape(1, 1, PAIR)
            diff = rebuilt - x_t[c, y // 2, :, y % 2, x].astype(F32)
            spot = pl.ds(pl.multiple_of(16 * tile, 16), 16)
            weight = loss_scale * keep[c, pl.ds(2 * (y // 2), 2), spot][:, :, :1]
            res[c, y // 2, :, y % 2, x] = (weight * diff).astype(BF16)

        step["sa", c] = spread_first(res, c, rs_s, rs_r)

    def residue_second(c):
        got(*step["sa", c])
        step["sb", c] = spread_second(res, c, rs_s, rs_r)

    def grad_dot(c):
        got(*step["sb", c])
        part = jnp.dot(rows_of(res, c), w_d[...].reshape(PAIR, 256), preferred_element_type=F32)
        g_f[c] = part.reshape(4, PADDED, 256)
        step["gc", c] = cross(c, 2, g_f, g_x)

    def grad_sum(c):
        got(step["gc", c])
        for q in (1, 2, 3):
            g_s[c, q - 1] = (g_f[c, q, :ROWS, mine] + g_x[c, q]).astype(BF16)
        step["gz", c] = z_group(2, lambda k: g_s.at[c, k - 1], lambda q: g_r.at[c, q - 1], c)
        g_own[c] = g_f[c, 0, :ROWS, mine] + g_x[c, 0]

    def grad_pre(c):
        if c == 0:
            got(step["cn"])
        got(*step["gz", c])
        norm_total = cnorm[0:1, mine] + cnorm_o[0:1, mine]
        grads = g_own[c] + loss_scale * SPARSITY * keep[c, 0, :ROWS] * norm_total
        for q in range(3):
            grads = grads + g_r[c, q].astype(F32)
        pg[c, 0, :ROWS, mine] = (grads * relu_slope(pre_own[c])).astype(BF16)
        step["qz", c] = z_group(3, lambda k: pg.at[c, 0, real, mine], lambda q: pg.at[c, q, real, mine], c)

    def grad_cross(c):
        got(*step["qz", c])
        step["qc", c] = cross_half(c, 3, pg)

    def dec_grad(c):
        f = rows_of(feat, c)
        active = jnp.sum(rows_of(keep, c)[:, :1] * f.astype(F32), axis=0, keepdims=True)
        penalty = loss_scale * SPARSITY * active / cnorm[0:1, :]
        total = w_d[...].reshape(PAIR, 256).astype(F32) * penalty + lax.dot_general(
            rows_of(res, c), f, (((0,), (0,)), ((), ())), preferred_element_type=F32
        )
        total = total.reshape(2, PAIR // 2, 256)
        dwd[...] = total if c == 0 else dwd[...] + total
        if c == CHUNKS - 1:
            dwd_s[...] = dwd[1 - r].astype(BF16)
            step["dwd"] = go(remote(dwd_s, dwd_r, one_s.at[3], one_r.at[3], twin))

    def enc_grad(c):
        got(step["qc", c])
        total = lax.dot_general(
            rows_of(x_t, c), rows_of(pg, c), (((0,), (0,)), ((), ())), preferred_element_type=F32
        ).reshape(2, PAIR // 2, 256)
        dwe[...] = total if c == 0 else dwe[...] + total
        if c == CHUNKS - 1:
            dwe_s[...] = dwe[1 - r].astype(BF16)
            step["dwe"] = go(remote(dwe_s, dwe_r, one_s.at[4], one_r.at[4], twin))

    stages = {
        "taps_first": taps_first,
        "taps_second": taps_second,
        "pre_dot": pre_dot,
        "pre_sum": pre_sum,
        "pre_act": pre_act,
        "feat_cross": feat_cross,
        "reb_dot": reb_dot,
        "reb_mid": reb_mid,
        "reb_sum": reb_sum,
        "residue": residue,
        "residue_second": residue_second,
        "grad_dot": grad_dot,
        "grad_sum": grad_sum,
        "grad_pre": grad_pre,
        "grad_cross": grad_cross,
        "enc_grad": enc_grad,
        "dec_grad": dec_grad,
        "norms_first": norms_first,
        "norms_second": norms_second,
    }
    for stage, c in ORDER:
        stages[stage](c)
    got(step["dwd"])
    dec_out[...] = (dwd[r] + dwd_r[...].astype(F32)).astype(BF16)
    got(step["dwe"])
    enc_out[...] = (dwe[r] + dwe_r[...].astype(F32)).astype(BF16)
    finish()


def local(taps, token_ids, enc_weight, enc_bias, dec_weight, dec_bias):
    tokens_dev = taps.shape[1]
    loss_scale = 1.0 / math.sqrt(tokens_dev * lax.axis_size("token"))
    c = CHUNKS
    dma = pltpu.SemaphoreType.DMA
    vmem = pltpu.VMEM
    tiles = (c, 2, 2, 2, 4, 16, PAIR)
    scratch = [
        vmem((1, tokens_dev), jnp.int32), vmem((1, 128), F32), vmem((1, PAIR), F32),
        vmem(tiles, BF16),
        vmem((2, 448, 256), BF16), vmem((2, 448, 256), BF16),
        vmem((4, 16, 224), BF16), vmem((c, 4, PADDED, 128), F32),
        vmem((4, 8, 256), F32), vmem((8, 256), F32), vmem((8, 256), F32),
        vmem((c, 4, PADDED, 256), F32), vmem((c, 4, ROWS, 128), F32),
        vmem((c, 3, ROWS, 128), BF16), vmem((c, 3, ROWS, 128), BF16), vmem((c, ROWS, 128), F32),
        vmem((c, 4, PADDED, 256), BF16),
        vmem(tiles, BF16),
        vmem((c, 3, 2, 2, 16, PAIR), BF16), vmem((c, 3, 4, 16, PAIR), BF16),
        vmem((c, 2, 2, 16, PAIR), BF16), vmem((c, 4, 16, PAIR), BF16),
        vmem((c, 2, 16, PAIR), BF16), vmem((c, 3, 2, 16, PAIR), BF16),
        vmem((c, 2, 16, PAIR), F32), vmem((c, 2, 16, PAIR), BF16), vmem((c, 2, 16, PAIR), BF16),
        vmem(tiles, BF16),
        vmem((c, 4, PADDED, 256), F32), vmem((c, 4, ROWS, 128), F32),
        vmem((c, 3, ROWS, 128), BF16), vmem((c, 3, ROWS, 128), BF16), vmem((c, ROWS, 128), F32),
        vmem((c, 4, PADDED, 256), BF16),
        vmem((2, 448, 256), F32), vmem((448, 256), BF16), vmem((448, 256), BF16),
        vmem((2, 448, 256), F32), vmem((448, 256), BF16), vmem((448, 256), BF16),
        dma((2 * c + 5,)),
        dma((c, 3)), dma((c, 3)), dma((2, c, 2, 3)), dma((2, c, 2, 3)),
        dma((3,)), dma((3,)), dma((3,)), dma((3,)),
        dma((5,)), dma((5,)),
        dma((4, c)), dma((4, c)), dma((4, c, 3)), dma((4, c, 3)),
        dma((2, c, 2, 3)), dma((2, c, 2, 3)), dma((c,)), dma((c,)), dma((2, c, 2, 3)), dma((2, c, 2, 3)),
    ]
    any_spec = pl.BlockSpec(memory_space=pl.ANY)
    vmem_spec = pl.BlockSpec(memory_space=pltpu.VMEM)
    enc_grad, dec_grad = pl.pallas_call(
        functools.partial(kernel, loss_scale),
        out_shape=(jax.ShapeDtypeStruct((448, 256), BF16), jax.ShapeDtypeStruct((448, 256), BF16)),
        in_specs=[any_spec] * 6,
        out_specs=(vmem_spec, vmem_spec),
        scratch_shapes=scratch,
        compiler_params=pltpu.CompilerParams(
            collective_id=0, has_side_effects=True, vmem_limit_bytes=60 * 1024 * 1024
        ),
        name="crosscoder",
    )(taps.reshape(tokens_dev // 16, 16, taps.shape[2]), token_ids[None, :], enc_weight[0], enc_bias[None, :], dec_weight[0], dec_bias)
    return enc_grad[None], dec_grad[None]


def solution(mesh):
    placed = (
        P("layer", "token", None),
        P("token"),
        P("layer", "token", "latent"),
        P("latent"),
        P("layer", "token", "latent"),
        P("layer", None),
    )
    return jax.shard_map(
        local,
        mesh=mesh,
        in_specs=placed,
        out_specs=(P("layer", "token", "latent"), P("layer", "token", "latent")),
        check_vma=False,
    )
```

time: 1120 us -> 143 us (0.13)
  waiting for transfers between devices: 1050 us -> 0 us
  Pallas kernels: 0 us -> 139 us
  blocking collectives: 23.9 us -> 0 us
  matrix products: 14.1 us -> 0 us
  between operations: 14.2 us -> 0.64 us
    psum x3 -> x0, waiting for transfers between devices: 781 us -> none  [the longest x1 692 us: local(): rebuilt = lax.psum(rebuilt_part, 'latent') + dec_bias[0][None, :]]
    pallas_call x0 -> x1, Pallas kernels: none -> 139 us  [local(): pl.pallas_call(functools.partial(kernel, loss_scale), out_shape=(jax.Shap...]
    all_gather x2 -> x0, waiting for transfers between devices: 137 us -> none  [the longest x1 72.1 us: local(): lax.all_gather(enc_weight[0], 'token', axis=0, tiled=True)]
    reduce_scatter x1 -> x0, waiting for transfers between devices: 68.7 us -> none  [local(): lax.psum_scatter((product + dec_full.astype(jnp.float32) * penalty_scale[...]
    unnamed x8 -> x0, waiting for transfers between devices: 63.7 us -> none
    psum x1 -> x0, blocking collectives: 23.9 us -> none  [local(): feat_back, norm_total = lax.psum((back_part, colnorm), 'layer')]
    dot_general x5 -> x0, matrix products: 14.1 us -> none  [the longest x1 3.92 us: local(): lax.dot_general(features, dec_full, (((1,), (1,)), ((), ())), preferred_e...]
  transfers between devices with their start and end apart: 7 -> 0, of which waited for: 7 -> 0; matrix products, arithmetic and copies ran while one was open for 1% -> 0% of each run, Pallas kernels for 0% -> 0%
where the time goes in v2:
time: 143 us
  Pallas kernels  139 us (97%)
  local copies, waits for them, and re-layouts  3.28 us (2%)
    pallas_call x1, Pallas kernels, local(): pl.pallas_call(functools.partial(kernel, loss_scale), out_shape=(jax.Shap...  139 us
    unnamed x2, local copies, waits for them, and re-layouts  3.28 us

profile of v2, /device:TPU:1, one launch (start us, length us, event | category | flops | bytes accessed | tf_op | source)
XLA Modules:
  0.0 142.8 jit_solution(2186983063778070693)
XLA Ops:
  0.6 138.8 %crosscoder.1 = (bf16[448,256]{1,0:T(8,128)(2,1)}, bf16[448,256]{1,0:T(8,128)(2,1)}) custom-call(bf16[14,16,3584]{2,1,0:T(8,128)(2,1)} %bitcast.7, s32[1,224]{1,0:T(1,128)} %bitcast.12, bf16[448,256]{1,0:T(8,128)(2,1)} %bitcast.10, f32[1,256]{1,0:T(1,128)} %bitcast.13, bf16[448,256]{1,0:T(8,128)(2,1)} %bitcast.11, f32[1,3584]{1,0:T(1,128)} %db.1), custom_call_target="tpu_custom_call" | custom-call | tf_op jit(solution)/shard_map/crosscoder/pallas_call | solution.py:458
  139.5 1.6 %copy.10 = bf16[1,448,256]{2,1,0:T(8,128)(2,1)} copy(bf16[1,448,256]{2,1,0:T(8,128)(2,1)} %bitcast.9) | data formatting | bytes 458752
  141.1 1.6 %copy.11 = bf16[1,448,256]{2,1,0:T(8,128)(2,1)} copy(bf16[1,448,256]{2,1,0:T(8,128)(2,1)} %bitcast.8) | data formatting | bytes 458752

commit v3 on v2

--- a/solution.py
+++ b/solution.py
@@ -21,16 +21,23 @@
 TILES = 7
 PAIR = 896
 
-CHAIN = (
-    "taps_first", "taps_second", "pre_dot", "pre_sum", "pre_act", "feat_cross", "reb_dot", "reb_mid", "reb_sum",
-    "residue", "residue_second", "grad_dot", "grad_sum", "dec_grad", "grad_pre", "grad_cross", "enc_grad",
+GROUPS = (
+    ("taps_first",), ("taps_second",), ("pre_dot", "pre_sum"), ("pre_act",), ("feat_cross", "reb_dot"), ("reb_mid",),
+    ("reb_sum",), ("residue",), ("residue_second",), ("grad_dot", "grad_sum"), ("grad_pre",), ("grad_cross", "enc_grad"),
 )
 LAG = 1
 ORDER = [
-    (stage, c) for _, c, stage in sorted((i + LAG * c, c, s) for i, s in enumerate(CHAIN) for c in range(CHUNKS))
+    (stage, c)
+    for _, c, g in sorted((g + LAG * c, c, g) for g in range(len(GROUPS)) for c in range(CHUNKS))
+    for stage in GROUPS[g]
 ]
-ORDER.insert(ORDER.index(("pre_sum", CHUNKS - 1)) + 1, ("norms_first", 0))
-ORDER.insert(ORDER.index(("reb_dot", 0)) + 1, ("norms_second", 0))
+for after, extra in (
+    (("grad_pre", CHUNKS - 1), [("dec_grad", c) for c in range(CHUNKS)]),
+    (("reb_dot", 0), [("norms_first", 0)]),
+    (("reb_sum", 0), [("norms_second", 0)]),
+):
+    spot = ORDER.index(after) + 1
+    ORDER[spot:spot] = extra
 
 
 def smooth_relu(preact):
@@ -46,8 +53,8 @@
 
 def kernel(loss_scale, taps, ids_in, we, eb, wd, db, enc_out, dec_out,
            ids, bias, dbias, x_t, w_e, w_d, mask, keep, nsq, cnorm, cnorm_o,
-           pre_f, pre_x, pre_s, pre_r, pre_own, feat, reb, row_r, col_r, row_s, col_s, own_s, end_r,
-           zs, zb, zr, res, g_f, g_x, g_s, g_r, g_own, pg, dwd, dwd_s, dwd_r, dwe, dwe_s, dwe_r,
+           pre_f, pre_o, pre_x, pre_s, pre_r, pre_own, feat, reb, row_r, col_r, row_s, col_s, own_s, end_r,
+           zs, zb, zr, res, g_f, g_o, g_x, g_s, g_r, g_own, pg, dwd, dwd_s, dwd_r, dwe, dwe_s, dwe_r,
            loc, xz_s, xz_r, xy_s, xy_r, mk_s, mk_r, ns_s, ns_r, one_s, one_r,
            co_s, co_r, zg_s, zg_r, rr_s, rr_r, zh_s, zh_r, rs_s, rs_r):
     layer = lax.axis_index("layer")
@@ -72,7 +79,7 @@
     def half(i):
         return pl.ds(pl.multiple_of(i * 128, 128), 128)
 
-    mine, theirs = half(layer), half(1 - layer)
+    mine = half(layer)
     cols = pl.ds(pl.multiple_of(p * PAIR, 128), PAIR)
     real = pl.ds(0, ROWS)
 
@@ -114,8 +121,9 @@
         pl.semaphore_signal(barrier, inc=1, device_id=dev, device_id_type=MESH)
     for c in range(CHUNKS):
         for q in range(4):
-            feat[c, q, ROWS:] = jnp.zeros((16, 256), BF16)
-            pg[c, q, ROWS:] = jnp.zeros((16, 256), BF16)
+            for i in range(2):
+                feat[c, i, q, ROWS:] = jnp.zeros((16, 128), BF16)
+                pg[c, i, q, ROWS:] = jnp.zeros((16, 128), BF16)
             keep[c, q, ROWS:] = jnp.zeros((16, 128), F32)
     ids_cp.wait()
     keep_row = (ids[...] != BEGIN_TOKEN).astype(F32)
@@ -199,14 +207,12 @@
         step["xa", c] = spread_first(x_t, c, xy_s, xy_r, low)
         if c == CHUNKS - 1:
             step["we"] = go(remote(we, w_e.at[r], one_s.at[0], one_r.at[0], twin))
-            step["wd"] = go(remote(wd, w_d.at[r], one_s.at[1], one_r.at[1], twin))
 
     def taps_second(c):
         got(*step["xa", c])
         step["xb", c] = spread_second(x_t, c, xy_s, xy_r, low)
 
     def norms_first(c):
-        got(step["wd"])
         w_sq = jnp.square(w_d[...].astype(F32)).reshape(PAIR, 256)
         nsq[0] = jnp.broadcast_to(jnp.sum(w_sq, axis=0, keepdims=True), (8, 256))
         step["ns"] = [
@@ -230,32 +236,38 @@
             for k in (1, 2, 3)
         ]
 
-    def cross(c, sem, full, got_ref):
-        return go(
-            remote(full.at[c, :, real, theirs], got_ref.at[c], co_s.at[sem, c], co_r.at[sem, c], other_core)
-        )
+    def cross(c, sem, part, own_ref, out_ref, got_ref):
+        part = part.reshape(4, PADDED, 256)[:, :ROWS]
+        is_low = layer == 0
+        own_ref[c] = jnp.where(is_low, part[:, :, :128], part[:, :, 128:])
+        out_ref[c] = jnp.where(is_low, part[:, :, 128:], part[:, :, :128]).astype(BF16)
+        return go(remote(out_ref.at[c], got_ref.at[c], co_s.at[sem, c], co_r.at[sem, c], other_core))
 
     def cross_half(c, sem, full):
-        block = full.at[c, :, real, mine]
+        block = full.at[c, layer, :, real]
         return go(remote(block, block, co_s.at[sem, c], co_r.at[sem, c], other_core))
 
     def rows_of(ref, c):
         return ref[c].reshape(4 * PADDED, ref.shape[-1])
+
+    def wide(ref, c):
+        return jnp.concatenate([ref[c, i].reshape(4 * PADDED, 128) for i in range(2)], axis=1)
 
     def pre_dot(c):
         got(*step["xb", c])
         if c == 0:
             got(step["we"])
         part = jnp.dot(rows_of(x_t, c), w_e[...].reshape(PAIR, 256), preferred_element_type=F32)
-        pre_f[c] = part.reshape(4, PADDED, 256)
-        step["pc", c] = cross(c, 0, pre_f, pre_x)
+        step["pc", c] = cross(c, 0, part, pre_f, pre_o, pre_x)
 
     def pre_sum(c):
         got(step["pc", c])
         for q in (1, 2, 3):
-            pre_s[c, q - 1] = (pre_f[c, q, :ROWS, mine] + pre_x[c, q]).astype(BF16)
+            pre_s[c, q - 1] = (pre_f[c, q] + pre_x[c, q].astype(F32)).astype(BF16)
         step["pz", c] = z_group(0, lambda k: pre_s.at[c, k - 1], lambda q: pre_r.at[c, q - 1], c)
-        pre_own[c] = pre_f[c, 0, :ROWS, mine] + pre_x[c, 0]
+        if c == 0:
+            step["wd"] = go(remote(wd, w_d.at[r], one_s.at[1], one_r.at[1], twin))
+        pre_own[c] = pre_f[c, 0] + pre_x[c, 0].astype(F32)
 
     def pre_act(c):
         got(*step["pz", c])
@@ -263,8 +275,8 @@
         for q in range(3):
             preact = preact + pre_r[c, q].astype(F32)
         pre_own[c] = preact
-        feat[c, 0, :ROWS, mine] = smooth_relu(preact).astype(BF16)
-        step["fz", c] = z_group(1, lambda k: feat.at[c, 0, real, mine], lambda q: feat.at[c, q, real, mine], c)
+        feat[c, layer, 0, :ROWS] = smooth_relu(preact).astype(BF16)
+        step["fz", c] = z_group(1, lambda k: feat.at[c, layer, 0, real], lambda q: feat.at[c, layer, q, real], c)
 
     def feat_cross(c):
         got(*step["fz", c])
@@ -272,8 +284,10 @@
 
     def reb_dot(c):
         got(step["fc", c])
+        if c == 0:
+            got(step["wd"])
         part = lax.dot_general(
-            rows_of(feat, c), w_d[...].reshape(PAIR, 256), (((1,), (1,)), ((), ())), preferred_element_type=F32
+            wide(feat, c), w_d[...].reshape(PAIR, 256), (((1,), (1,)), ((), ())), preferred_element_type=F32
         )
         reb[c] = part.astype(BF16).reshape(2, 2, 2, 4, 16, PAIR)
         step["ra", c] = []
@@ -341,15 +355,14 @@
     def grad_dot(c):
         got(*step["sb", c])
         part = jnp.dot(rows_of(res, c), w_d[...].reshape(PAIR, 256), preferred_element_type=F32)
-        g_f[c] = part.reshape(4, PADDED, 256)
-        step["gc", c] = cross(c, 2, g_f, g_x)
+        step["gc", c] = cross(c, 2, part, g_f, g_o, g_x)
 
     def grad_sum(c):
         got(step["gc", c])
         for q in (1, 2, 3):
-            g_s[c, q - 1] = (g_f[c, q, :ROWS, mine] + g_x[c, q]).astype(BF16)
+            g_s[c, q - 1] = (g_f[c, q] + g_x[c, q].astype(F32)).astype(BF16)
         step["gz", c] = z_group(2, lambda k: g_s.at[c, k - 1], lambda q: g_r.at[c, q - 1], c)
-        g_own[c] = g_f[c, 0, :ROWS, mine] + g_x[c, 0]
+        g_own[c] = g_f[c, 0] + g_x[c, 0].astype(F32)
 
     def grad_pre(c):
         if c == 0:
@@ -359,15 +372,15 @@
         grads = g_own[c] + loss_scale * SPARSITY * keep[c, 0, :ROWS] * norm_total
         for q in range(3):
             grads = grads + g_r[c, q].astype(F32)
-        pg[c, 0, :ROWS, mine] = (grads * relu_slope(pre_own[c])).astype(BF16)
-        step["qz", c] = z_group(3, lambda k: pg.at[c, 0, real, mine], lambda q: pg.at[c, q, real, mine], c)
+        pg[c, layer, 0, :ROWS] = (grads * relu_slope(pre_own[c])).astype(BF16)
+        step["qz", c] = z_group(3, lambda k: pg.at[c, layer, 0, real], lambda q: pg.at[c, layer, q, real], c)
 
     def grad_cross(c):
         got(*step["qz", c])
         step["qc", c] = cross_half(c, 3, pg)
 
     def dec_grad(c):
-        f = rows_of(feat, c)
+        f = wide(feat, c)
         active = jnp.sum(rows_of(keep, c)[:, :1] * f.astype(F32), axis=0, keepdims=True)
         penalty = loss_scale * SPARSITY * active / cnorm[0:1, :]
         total = w_d[...].reshape(PAIR, 256).astype(F32) * penalty + lax.dot_general(
@@ -382,7 +395,7 @@
     def enc_grad(c):
         got(step["qc", c])
         total = lax.dot_general(
-            rows_of(x_t, c), rows_of(pg, c), (((0,), (0,)), ((), ())), preferred_element_type=F32
+            rows_of(x_t, c), wide(pg, c), (((0,), (0,)), ((), ())), preferred_element_type=F32
         ).reshape(2, PAIR // 2, 256)
         dwe[...] = total if c == 0 else dwe[...] + total
         if c == CHUNKS - 1:
@@ -432,18 +445,18 @@
         vmem((2, 448, 256), BF16), vmem((2, 448, 256), BF16),
         vmem((4, 16, 224), BF16), vmem((c, 4, PADDED, 128), F32),
         vmem((4, 8, 256), F32), vmem((8, 256), F32), vmem((8, 256), F32),
-        vmem((c, 4, PADDED, 256), F32), vmem((c, 4, ROWS, 128), F32),
+        vmem((c, 4, ROWS, 128), F32), vmem((c, 4, ROWS, 128), BF16), vmem((c, 4, ROWS, 128), BF16),
         vmem((c, 3, ROWS, 128), BF16), vmem((c, 3, ROWS, 128), BF16), vmem((c, ROWS, 128), F32),
-        vmem((c, 4, PADDED, 256), BF16),
+        vmem((c, 2, 4, PADDED, 128), BF16),
         vmem(tiles, BF16),
         vmem((c, 3, 2, 2, 16, PAIR), BF16), vmem((c, 3, 4, 16, PAIR), BF16),
         vmem((c, 2, 2, 16, PAIR), BF16), vmem((c, 4, 16, PAIR), BF16),
         vmem((c, 2, 16, PAIR), BF16), vmem((c, 3, 2, 16, PAIR), BF16),
         vmem((c, 2, 16, PAIR), F32), vmem((c, 2, 16, PAIR), BF16), vmem((c, 2, 16, PAIR), BF16),
         vmem(tiles, BF16),
-        vmem((c, 4, PADDED, 256), F32), vmem((c, 4, ROWS, 128), F32),
+        vmem((c, 4, ROWS, 128), F32), vmem((c, 4, ROWS, 128), BF16), vmem((c, 4, ROWS, 128), BF16),
         vmem((c, 3, ROWS, 128), BF16), vmem((c, 3, ROWS, 128), BF16), vmem((c, ROWS, 128), F32),
-        vmem((c, 4, PADDED, 256), BF16),
+        vmem((c, 2, 4, PADDED, 128), BF16),
         vmem((2, 448, 256), F32), vmem((448, 256), BF16), vmem((448, 256), BF16),
         vmem((2, 448, 256), F32), vmem((448, 256), BF16), vmem((448, 256), BF16),
         dma((2 * c + 5,)),

time: 143 us -> 132 us (0.923)
  Pallas kernels: 139 us -> 128 us
    pallas_call x1, Pallas kernels: 139 us -> 128 us  [local(): pl.pallas_call(functools.partial(kernel, loss_scale), out_shape=(jax.Shap...]
where the time goes in v3:
time: 132 us
  Pallas kernels  128 us (97%)
  local copies, waits for them, and re-layouts  3.28 us (2%)
    pallas_call x1, Pallas kernels, local(): pl.pallas_call(functools.partial(kernel, loss_scale), out_shape=(jax.Shap...  128 us
    unnamed x2, local copies, waits for them, and re-layouts  3.28 us

profile of v3, /device:TPU:1, one launch (start us, length us, event | category | flops | bytes accessed | tf_op | source)
XLA Modules:
  0.0 132.3 jit_solution(1908170387937572263)
XLA Ops:
  0.6 128.4 %crosscoder.1 = (bf16[448,256]{1,0:T(8,128)(2,1)}, bf16[448,256]{1,0:T(8,128)(2,1)}) custom-call(bf16[14,16,3584]{2,1,0:T(8,128)(2,1)} %bitcast.7, s32[1,224]{1,0:T(1,128)} %bitcast.12, bf16[448,256]{1,0:T(8,128)(2,1)} %bitcast.10, f32[1,256]{1,0:T(1,128)} %bitcast.13, bf16[448,256]{1,0:T(8,128)(2,1)} %bitcast.11, f32[1,3584]{1,0:T(1,128)} %db.1), custom_call_target="tpu_custom_call" | custom-call | tf_op jit(solution)/shard_map/crosscoder/pallas_call | solution.py:471
  129.0 1.6 %copy.10 = bf16[1,448,256]{2,1,0:T(8,128)(2,1)} copy(bf16[1,448,256]{2,1,0:T(8,128)(2,1)} %bitcast.9) | data formatting | bytes 458752
  130.6 1.6 %copy.11 = bf16[1,448,256]{2,1,0:T(8,128)(2,1)} copy(bf16[1,448,256]{2,1,0:T(8,128)(2,1)} %bitcast.8) | data formatting | bytes 458752

commit v4 on v3

--- a/solution.py
+++ b/solution.py
@@ -22,8 +22,19 @@
 PAIR = 896
 
 GROUPS = (
-    ("taps_first",), ("taps_second",), ("pre_dot", "pre_sum"), ("pre_act",), ("feat_cross", "reb_dot"), ("reb_mid",),
-    ("reb_sum",), ("residue",), ("residue_second",), ("grad_dot", "grad_sum"), ("grad_pre",), ("grad_cross", "enc_grad"),
+    ("taps_first",),
+    ("taps_second",),
+    ("pre_dot", "pre_sum",),
+    ("pre_act",),
+    ("feat_cross",),
+    ("reb_dot",),
+    ("reb_mid",),
+    ("reb_sum",),
+    ("residue",),
+    ("residue_second",),
+    ("grad_dot", "grad_sum",),
+    ("grad_pre",),
+    ("grad_cross", "enc_grad",),
 )
 LAG = 1
 ORDER = [
@@ -205,8 +216,10 @@
     def taps_first(c):
         got(*step["xz", c])
         step["xa", c] = spread_first(x_t, c, xy_s, xy_r, low)
+        if c == 0:
+            step["we"] = go(remote(we, w_e.at[r], one_s.at[0], one_r.at[0], twin))
         if c == CHUNKS - 1:
-            step["we"] = go(remote(we, w_e.at[r], one_s.at[0], one_r.at[0], twin))
+            step["wd"] = go(remote(wd, w_d.at[r], one_s.at[1], one_r.at[1], twin))
 
     def taps_second(c):
         got(*step["xa", c])
@@ -265,8 +278,6 @@
         for q in (1, 2, 3):
             pre_s[c, q - 1] = (pre_f[c, q] + pre_x[c, q].astype(F32)).astype(BF16)
         step["pz", c] = z_group(0, lambda k: pre_s.at[c, k - 1], lambda q: pre_r.at[c, q - 1], c)
-        if c == 0:
-            step["wd"] = go(remote(wd, w_d.at[r], one_s.at[1], one_r.at[1], twin))
         pre_own[c] = pre_f[c, 0] + pre_x[c, 0].astype(F32)
 
     def pre_act(c):

time: 132 us -> 131 us (level)
  no operation moved by 1% of the time
where the time goes in v4:
time: 131 us
  Pallas kernels  127 us (97%)
  local copies, waits for them, and re-layouts  3.28 us (3%)
    pallas_call x1, Pallas kernels, local(): pl.pallas_call(functools.partial(kernel, loss_scale), out_shape=(jax.Shap...  127 us
    unnamed x2, local copies, waits for them, and re-layouts  3.28 us

profile of v4, /device:TPU:1, one launch (start us, length us, event | category | flops | bytes accessed | tf_op | source)
XLA Modules:
  0.0 131.2 jit_solution(6068061191459084377)
XLA Ops:
  0.6 127.3 %crosscoder.1 = (bf16[448,256]{1,0:T(8,128)(2,1)}, bf16[448,256]{1,0:T(8,128)(2,1)}) custom-call(bf16[14,16,3584]{2,1,0:T(8,128)(2,1)} %bitcast.7, s32[1,224]{1,0:T(1,128)} %bitcast.12, bf16[448,256]{1,0:T(8,128)(2,1)} %bitcast.10, f32[1,256]{1,0:T(1,128)} %bitcast.13, bf16[448,256]{1,0:T(8,128)(2,1)} %bitcast.11, f32[1,3584]{1,0:T(1,128)} %db.1), custom_call_target="tpu_custom_call" | custom-call | tf_op jit(solution)/shard_map/crosscoder/pallas_call | solution.py:482
  128.0 1.6 %copy.10 = bf16[1,448,256]{2,1,0:T(8,128)(2,1)} copy(bf16[1,448,256]{2,1,0:T(8,128)(2,1)} %bitcast.9) | data formatting | bytes 458752
  129.6 1.6 %copy.11 = bf16[1,448,256]{2,1,0:T(8,128)(2,1)} copy(bf16[1,448,256]{2,1,0:T(8,128)(2,1)} %bitcast.8) | data formatting | bytes 458752
